TPU v7x, 256 devices: a whole 4x4x8 slice. The times are simulated.
256 devices in a mesh: samp: 32 (over z, y), rows: 8 (over x, core).
Axes of the slice: x: 4, y: 4, z: 8, core: 2. Of those that a mesh axis runs over, the one named last changes fastest.
Arguments:
- samples: float32 [32, 640, 4480], P('samp', 'rows'), may hold values from -6 to 6
- truth_field: float32 [640, 4480], P('rows', 'samp'), may hold values from -6 to 6
Outputs:
- contrast_fine: float32 [32, 640, 4480], P('samp', 'rows')
- contrast_half: float32 [32, 320, 2240], P('samp', 'rows')
- contrast_quarter: float32 [32, 160, 1120], P('samp', 'rows')
- contrast_eighth: float32 [32, 80, 560], P('samp', 'rows')
- similarity_coarse: float32 [32, 40, 280], P('samp', 'rows')
All inputs are finite; a program needn't handle non-finite values.
Results may differ from a plain program's by a relative error of at most 0.00002.
Values sent between devices are 32-bit elements; how exact they have to be, the bound alone decides.
No kernel may reach another device: no remote copies, remote signals or barrier semaphores. Data moves between devices by JAX's collectives and lax.ppermute only.
A program may use at most 128 MiB of HBM per device.

v0:
```python
import jax
import jax.numpy as jnp
from jax import lax
from jax.sharding import PartitionSpec as P

small_one = 0.0001
small_two = 0.0009


def with_halo(block, sides, width):
    for axis, dim in sides:
        count = lax.axis_size(axis)
        forward = [(i, i + 1) for i in range(count - 1)]
        backward = [(target, source) for source, target in forward]
        low = lax.ppermute(
            lax.slice_in_dim(block, block.shape[dim] - width, None, axis=dim), axis, forward
        )
        high = lax.ppermute(lax.slice_in_dim(block, 0, width, axis=dim), axis, backward)
        block = jnp.concatenate([low, block, high], axis=dim)
    return block


def window():
    offsets = jnp.arange(11).astype(jnp.float32) - 5.0
    shaped = jnp.exp(-offsets * offsets / 4.5)
    return shaped / jnp.sum(shaped)


def smooth(padded, weights):
    row_count = padded.shape[-2] - 10
    column_count = padded.shape[-1]
    vertical = weights[0] * padded[..., 0:row_count, :]
    for tap_index in range(1, 11):
        vertical = vertical + weights[tap_index] * padded[..., tap_index : tap_index + row_count, :]
    widths = [(0, 0)] * (padded.ndim - 1) + [(5, 5)]
    widened = jnp.pad(vertical, widths)
    result = weights[0] * widened[..., 0:column_count]
    for tap_index in range(1, 11):
        result = result + weights[tap_index] * widened[..., tap_index : tap_index + column_count]
    return result


def halve_grid(field):
    upper = field[..., 0::2, :]
    lower = field[..., 1::2, :]
    return 0.25 * (upper[..., 0::2] + upper[..., 1::2] + lower[..., 0::2] + lower[..., 1::2])


def level_maps(sample_pad, truth_pad, weights, coarsest):
    truth_wide = truth_pad[None]
    stacked = jnp.stack(
        [
            sample_pad,
            truth_wide,
            sample_pad * sample_pad,
            truth_wide * truth_wide,
            sample_pad * truth_wide,
        ],
        axis=0,
    )
    moments = lax.map(lambda field: smooth(field, weights), stacked)
    mean_x = moments[0]
    mean_y = moments[1]
    var_x = moments[2] - mean_x * mean_x
    var_y = moments[3] - mean_y * mean_y
    covar = moments[4] - mean_x * mean_y
    contrast = (2.0 * covar + small_two) / (var_x + var_y + small_two)
    if coarsest:
        luminance = (2.0 * mean_x * mean_y + small_one) / (
            mean_x * mean_x + mean_y * mean_y + small_one
        )
        return luminance * contrast
    return contrast


def local(samples, truth_field):
    weights = window()
    truth_levels = []
    sample_levels = []
    truth_rows = lax.all_gather(truth_field, "samp", axis=1, tiled=True)
    current = jnp.concatenate([truth_rows[None], samples], axis=0)
    for level_index in range(5):
        if level_index > 0:
            current = halve_grid(current)
        padded = with_halo(current, (("rows", 1),), 5)
        truth_levels.append(padded[0])
        sample_levels.append(padded[1:])
    return tuple(
        (
            level_maps(
                sample_levels[level_index], truth_levels[level_index], weights, level_index == 4
            )
            for level_index in range(5)
        )
    )


def solution(mesh):
    placed = (P("samp", "rows", None), P("rows", "samp"))
    return jax.shard_map(
        local,
        mesh=mesh,
        in_specs=placed,
        out_specs=(
            P("samp", "rows", None),
            P("samp", "rows", None),
            P("samp", "rows", None),
            P("samp", "rows", None),
            P("samp", "rows", None),
        ),
        check_vma=False,
    )
```

profile of v0, /device:TPU:1, one launch (start us, length us, event | category | flops | bytes accessed | tf_op | source)
XLA Modules:
  0.0 804.6 jit_solution(12436675204161090629)
XLA Ops:
  9.2 80.0 %all-gather.3.cloned.1.call-done = f32[32,140,80]{2,1,0:T(8,128)} async-done(((f32[1,140,80]{2,1,0:T(8,128)}), f32[32,140,80]{2,1,0:T(8,128)}) %all-gather.3.cloned.1.call-update) | async-done | bytes 1433616 | tf_op jit(solution)/shard_map/all_gather | solution.py:80
  96.0 7.6 slice.1230
  103.6 30.2 %slice.1231 = f32[2,40,2240]{2,1,0:T(8,128)} slice(f32[2,40,4480]{2,1,0:T(8,128)} %slice.1230), slice={[0:2:1], [0:40:1], [0:4480:2]} | slice | bytes 1433600 | tf_op jit(solution)/shard_map/slice | solution.py:46
  133.8 30.2 %slice.1232 = f32[2,40,2240]{2,1,0:T(8,128)} slice(f32[2,40,4480]{2,1,0:T(8,128)} %slice.1230), slice={[0:2:1], [0:40:1], [1:4480:2]} | slice | bytes 1433600 | tf_op jit(solution)/shard_map/slice | solution.py:46
  164.0 7.6 slice.1233
  171.6 30.4 %slice.1234 = f32[2,40,2240]{2,1,0:T(8,128)} slice(f32[2,40,4480]{2,1,0:T(8,128)} %slice.1233), slice={[0:2:1], [0:40:1], [0:4480:2]} | slice | bytes 1433600 | tf_op jit(solution)/shard_map/slice | solution.py:46
  201.9 30.2 %slice.1235 = f32[2,40,2240]{2,1,0:T(8,128)} slice(f32[2,40,4480]{2,1,0:T(8,128)} %slice.1233), slice={[0:2:1], [0:40:1], [1:4480:2]} | slice | bytes 1433600 | tf_op jit(solution)/shard_map/slice | solution.py:46
  277.0 7.2 collective-permute-start.8
  304.2 80.6 %while.64 = (s32[]{:T(128)}, f32[5,1,5,280]{3,0,2,1:T(8,128)}, f32[11]{0:T(128)S(1)}, f32[5,1,15,280]{3,2,1,0:T(8,128)S(1)}, s32[]{:T(128)}, /*index=5*/s32[]{:T(128)}) while((s32[]{:T(128)}, f32[5,1,5,280]{3,0,2,1:T(8,128)}, f32[11]{0:T(128)S(1)}, f32[5,1,15,280]{3,2,1,0:T(8,128)S(1)}, s32[]{:T(128)}, /*index=5*/s32[]{:T(128)}) %tuple.190), condition=%wide.region_10.11_spmd, body=%wide.region_9.10_spmd.sunk | while | flops 58802 | bytes 134653 | solution.py:61
  392.2 83.3 %while.63 = (s32[]{:T(128)}, f32[5,1,10,560]{3,0,2,1:T(8,128)}, f32[11]{0:T(128)S(1)}, f32[5,1,20,560]{3,2,1,0:T(8,128)S(1)}, s32[]{:T(128)}, /*index=5*/s32[]{:T(128)}) while((s32[]{:T(128)}, f32[5,1,10,560]{3,0,2,1:T(8,128)}, f32[11]{0:T(128)S(1)}, f32[5,1,20,560]{3,2,1,0:T(8,128)S(1)}, s32[]{:T(128)}, /*index=5*/s32[]{:T(128)}) %tuple.195), condition=%wide.region_8.9_spmd, body=%wide.region_7.8_spmd.sunk | while | flops 235202 | bytes 493053 | solution.py:61
  392.9 7.0 fusion.127
  400.0 7.2 add_bitcast_fusion.7
  409.6 7.0 fusion.127
  416.6 7.2 add_bitcast_fusion.7
  426.2 7.0 fusion.127
  433.3 7.2 add_bitcast_fusion.7
  442.9 7.0 fusion.127
  449.9 7.2 add_bitcast_fusion.7
  459.5 7.0 fusion.127
  466.6 7.2 add_bitcast_fusion.7
  481.6 94.7 %while.62 = (s32[]{:T(128)}, f32[5,1,20,1120]{3,0,2,1:T(8,128)}, f32[11]{0:T(128)S(1)}, f32[5,1,30,1120]{3,2,1,0:T(8,128)}, s32[]{:T(128)}, /*index=5*/s32[]{:T(128)}) while((s32[]{:T(128)}, f32[5,1,20,1120]{3,0,2,1:T(8,128)}, f32[11]{0:T(128)S(1)}, f32[5,1,30,1120]{3,2,1,0:T(8,128)}, s32[]{:T(128)}, /*index=5*/s32[]{:T(128)}) %tuple.201), condition=%wide.region_6.7_spmd, body=%wide.region_5.6_spmd.sunk | while | flops 940802 | bytes 1881853 | solution.py:61
  490.4 7.2 add_bitcast_fusion.6
  509.3 7.2 add_bitcast_fusion.6
  528.2 7.2 add_bitcast_fusion.6
  547.1 7.2 add_bitcast_fusion.6
  565.9 7.2 add_bitcast_fusion.6
  582.8 90.1 %while.61 = (s32[]{:T(128)}, f32[5,1,40,2240]{3,2,1,0:T(8,128)}, f32[11]{0:T(128)S(1)}, f32[5,1,50,2240]{3,2,1,0:T(8,128)}, s32[]{:T(128)}) while((s32[]{:T(128)}, f32[5,1,40,2240]{3,2,1,0:T(8,128)}, f32[11]{0:T(128)S(1)}, f32[5,1,50,2240]{3,2,1,0:T(8,128)}, s32[]{:T(128)}) %tuple.200), condition=%wide.region_4.5_spmd, body=%wide.region_3.4_spmd.sunk | while | flops 3763202 | bytes 5930181 | solution.py:61
  584.6 7.5 fusion.123
  592.0 8.8 %bitcast_dynamic-update-slice_fusion.25 = f32[5,1,40,2240]{3,2,1,0:T(8,128)} fusion(f32[5,1,40,2240]{3,2,1,0:T(8,128)} %get-tuple-element.634, s32[]{:T(128)} %get-tuple-element.633, f32[1,40,2240]{2,1,0:T(8,128)S(1)} %fusion.123, f32[]{:T(128)} %bitcast.279, f32[]{:T(128)} %bitcast.280, f32[]{:T(128)} %bitcast.281, f32[]{:T(128)} %bitcast.282, ...), kind=kLoop, calls=%fused_computation.56.clone.1 | loop fusion | flops 1881600 | bytes 733184 | tf_op jit(solution)/shard_map/while/body/jit(dynamic_update_index_in_dim)/dynamic_update_slice | solution.py:61
  602.6 7.5 fusion.123
  610.0 8.8 %bitcast_dynamic-update-slice_fusion.25 = f32[5,1,40,2240]{3,2,1,0:T(8,128)} fusion(f32[5,1,40,2240]{3,2,1,0:T(8,128)} %get-tuple-element.634, s32[]{:T(128)} %get-tuple-element.633, f32[1,40,2240]{2,1,0:T(8,128)S(1)} %fusion.123, f32[]{:T(128)} %bitcast.279, f32[]{:T(128)} %bitcast.280, f32[]{:T(128)} %bitcast.281, f32[]{:T(128)} %bitcast.282, ...), kind=kLoop, calls=%fused_computation.56.clone.1 | loop fusion | flops 1881600 | bytes 733184 | tf_op jit(solution)/shard_map/while/body/jit(dynamic_update_index_in_dim)/dynamic_update_slice | solution.py:61
  620.6 7.5 fusion.123
  628.0 8.8 %bitcast_dynamic-update-slice_fusion.25 = f32[5,1,40,2240]{3,2,1,0:T(8,128)} fusion(f32[5,1,40,2240]{3,2,1,0:T(8,128)} %get-tuple-element.634, s32[]{:T(128)} %get-tuple-element.633, f32[1,40,2240]{2,1,0:T(8,128)S(1)} %fusion.123, f32[]{:T(128)} %bitcast.279, f32[]{:T(128)} %bitcast.280, f32[]{:T(128)} %bitcast.281, f32[]{:T(128)} %bitcast.282, ...), kind=kLoop, calls=%fused_computation.56.clone.1 | loop fusion | flops 1881600 | bytes 733184 | tf_op jit(solution)/shard_map/while/body/jit(dynamic_update_index_in_dim)/dynamic_update_slice | solution.py:61
  638.6 7.5 fusion.123
  646.1 8.8 %bitcast_dynamic-update-slice_fusion.25 = f32[5,1,40,2240]{3,2,1,0:T(8,128)} fusion(f32[5,1,40,2240]{3,2,1,0:T(8,128)} %get-tuple-element.634, s32[]{:T(128)} %get-tuple-element.633, f32[1,40,2240]{2,1,0:T(8,128)S(1)} %fusion.123, f32[]{:T(128)} %bitcast.279, f32[]{:T(128)} %bitcast.280, f32[]{:T(128)} %bitcast.281, f32[]{:T(128)} %bitcast.282, ...), kind=kLoop, calls=%fused_computation.56.clone.1 | loop fusion | flops 1881600 | bytes 733184 | tf_op jit(solution)/shard_map/while/body/jit(dynamic_update_index_in_dim)/dynamic_update_slice | solution.py:61
  656.6 7.5 fusion.123
  664.1 8.8 %bitcast_dynamic-update-slice_fusion.25 = f32[5,1,40,2240]{3,2,1,0:T(8,128)} fusion(f32[5,1,40,2240]{3,2,1,0:T(8,128)} %get-tuple-element.634, s32[]{:T(128)} %get-tuple-element.633, f32[1,40,2240]{2,1,0:T(8,128)S(1)} %fusion.123, f32[]{:T(128)} %bitcast.279, f32[]{:T(128)} %bitcast.280, f32[]{:T(128)} %bitcast.281, f32[]{:T(128)} %bitcast.282, ...), kind=kLoop, calls=%fused_computation.56.clone.1 | loop fusion | flops 1881600 | bytes 733184 | tf_op jit(solution)/shard_map/while/body/jit(dynamic_update_index_in_dim)/dynamic_update_slice | solution.py:61
  680.5 112.1 %while.60 = (s32[]{:T(128)}, f32[5,1,80,4480]{3,2,1,0:T(8,128)}, f32[11]{0:T(128)S(1)}, f32[5,1,90,4480]{3,2,1,0:T(8,128)}, s32[]{:T(128)}) while((s32[]{:T(128)}, f32[5,1,80,4480]{3,2,1,0:T(8,128)}, f32[11]{0:T(128)S(1)}, f32[5,1,90,4480]{3,2,1,0:T(8,128)}, s32[]{:T(128)}) %tuple.199), condition=%wide.region_2.3_spmd, body=%wide.region_1.2_spmd.sunk | while | flops 15052802 | bytes 23302340 | solution.py:61
  682.7 8.7 %fusion.121 = f32[1,80,4480]{2,1,0:T(8,128)S(1)} fusion(f32[1,90,4480]{2,1,0:T(8,128)S(1)} %dynamic-slice_bitcast_fusion.10, f32[]{:T(128)} %bitcast.266, f32[]{:T(128)} %bitcast.267, f32[]{:T(128)} %bitcast.268, f32[]{:T(128)} %bitcast.269, f32[]{:T(128)} %bitcast.270, f32[]{:T(128)} %bitcast.271, f32[]{:T(128)} %bitcast.272, f32[]{:T(128)} %bitcast.273, ...), kind=kLoop, calls=%fused_computation.2.clone.1 | loop fusion | flops 7526400 | bytes 17203244 | tf_op jit(solution)/shard_map/while/body/eval_jaxpr/add | solution.py:34
  691.4 11.5 %bitcast_dynamic-update-slice_fusion.24 = f32[5,1,80,4480]{3,2,1,0:T(8,128)} fusion(f32[5,1,80,4480]{3,2,1,0:T(8,128)} %get-tuple-element.619, s32[]{:T(128)} %get-tuple-element.618, f32[1,80,4480]{2,1,0:T(8,128)S(1)} %fusion.121, f32[]{:T(128)} %bitcast.266, f32[]{:T(128)} %bitcast.267, f32[]{:T(128)} %bitcast.268, f32[]{:T(128)} %bitcast.269, ...), kind=kLoop, calls=%fused_computation.22.clone.1 | loop fusion | flops 7526400 | bytes 2873344 | tf_op jit(solution)/shard_map/while/body/jit(dynamic_update_index_in_dim)/dynamic_update_slice | solution.py:61
  705.2 8.7 %fusion.121 = f32[1,80,4480]{2,1,0:T(8,128)S(1)} fusion(f32[1,90,4480]{2,1,0:T(8,128)S(1)} %dynamic-slice_bitcast_fusion.10, f32[]{:T(128)} %bitcast.266, f32[]{:T(128)} %bitcast.267, f32[]{:T(128)} %bitcast.268, f32[]{:T(128)} %bitcast.269, f32[]{:T(128)} %bitcast.270, f32[]{:T(128)} %bitcast.271, f32[]{:T(128)} %bitcast.272, f32[]{:T(128)} %bitcast.273, ...), kind=kLoop, calls=%fused_computation.2.clone.1 | loop fusion | flops 7526400 | bytes 17203244 | tf_op jit(solution)/shard_map/while/body/eval_jaxpr/add | solution.py:34
  713.9 11.5 %bitcast_dynamic-update-slice_fusion.24 = f32[5,1,80,4480]{3,2,1,0:T(8,128)} fusion(f32[5,1,80,4480]{3,2,1,0:T(8,128)} %get-tuple-element.619, s32[]{:T(128)} %get-tuple-element.618, f32[1,80,4480]{2,1,0:T(8,128)S(1)} %fusion.121, f32[]{:T(128)} %bitcast.266, f32[]{:T(128)} %bitcast.267, f32[]{:T(128)} %bitcast.268, f32[]{:T(128)} %bitcast.269, ...), kind=kLoop, calls=%fused_computation.22.clone.1 | loop fusion | flops 7526400 | bytes 2873344 | tf_op jit(solution)/shard_map/while/body/jit(dynamic_update_index_in_dim)/dynamic_update_slice | solution.py:61
  727.6 8.7 %fusion.121 = f32[1,80,4480]{2,1,0:T(8,128)S(1)} fusion(f32[1,90,4480]{2,1,0:T(8,128)S(1)} %dynamic-slice_bitcast_fusion.10, f32[]{:T(128)} %bitcast.266, f32[]{:T(128)} %bitcast.267, f32[]{:T(128)} %bitcast.268, f32[]{:T(128)} %bitcast.269, f32[]{:T(128)} %bitcast.270, f32[]{:T(128)} %bitcast.271, f32[]{:T(128)} %bitcast.272, f32[]{:T(128)} %bitcast.273, ...), kind=kLoop, calls=%fused_computation.2.clone.1 | loop fusion | flops 7526400 | bytes 17203244 | tf_op jit(solution)/shard_map/while/body/eval_jaxpr/add | solution.py:34
  736.3 11.5 %bitcast_dynamic-update-slice_fusion.24 = f32[5,1,80,4480]{3,2,1,0:T(8,128)} fusion(f32[5,1,80,4480]{3,2,1,0:T(8,128)} %get-tuple-element.619, s32[]{:T(128)} %get-tuple-element.618, f32[1,80,4480]{2,1,0:T(8,128)S(1)} %fusion.121, f32[]{:T(128)} %bitcast.266, f32[]{:T(128)} %bitcast.267, f32[]{:T(128)} %bitcast.268, f32[]{:T(128)} %bitcast.269, ...), kind=kLoop, calls=%fused_computation.22.clone.1 | loop fusion | flops 7526400 | bytes 2873344 | tf_op jit(solution)/shard_map/while/body/jit(dynamic_update_index_in_dim)/dynamic_update_slice | solution.py:61
  750.0 8.7 %fusion.121 = f32[1,80,4480]{2,1,0:T(8,128)S(1)} fusion(f32[1,90,4480]{2,1,0:T(8,128)S(1)} %dynamic-slice_bitcast_fusion.10, f32[]{:T(128)} %bitcast.266, f32[]{:T(128)} %bitcast.267, f32[]{:T(128)} %bitcast.268, f32[]{:T(128)} %bitcast.269, f32[]{:T(128)} %bitcast.270, f32[]{:T(128)} %bitcast.271, f32[]{:T(128)} %bitcast.272, f32[]{:T(128)} %bitcast.273, ...), kind=kLoop, calls=%fused_computation.2.clone.1 | loop fusion | flops 7526400 | bytes 17203244 | tf_op jit(solution)/shard_map/while/body/eval_jaxpr/add | solution.py:34
  758.7 11.5 %bitcast_dynamic-update-slice_fusion.24 = f32[5,1,80,4480]{3,2,1,0:T(8,128)} fusion(f32[5,1,80,4480]{3,2,1,0:T(8,128)} %get-tuple-element.619, s32[]{:T(128)} %get-tuple-element.618, f32[1,80,4480]{2,1,0:T(8,128)S(1)} %fusion.121, f32[]{:T(128)} %bitcast.266, f32[]{:T(128)} %bitcast.267, f32[]{:T(128)} %bitcast.268, f32[]{:T(128)} %bitcast.269, ...), kind=kLoop, calls=%fused_computation.22.clone.1 | loop fusion | flops 7526400 | bytes 2873344 | tf_op jit(solution)/shard_map/while/body/jit(dynamic_update_index_in_dim)/dynamic_update_slice | solution.py:61
  772.5 8.7 %fusion.121 = f32[1,80,4480]{2,1,0:T(8,128)S(1)} fusion(f32[1,90,4480]{2,1,0:T(8,128)S(1)} %dynamic-slice_bitcast_fusion.10, f32[]{:T(128)} %bitcast.266, f32[]{:T(128)} %bitcast.267, f32[]{:T(128)} %bitcast.268, f32[]{:T(128)} %bitcast.269, f32[]{:T(128)} %bitcast.270, f32[]{:T(128)} %bitcast.271, f32[]{:T(128)} %bitcast.272, f32[]{:T(128)} %bitcast.273, ...), kind=kLoop, calls=%fused_computation.2.clone.1 | loop fusion | flops 7526400 | bytes 17203244 | tf_op jit(solution)/shard_map/while/body/eval_jaxpr/add | solution.py:34
  781.2 11.5 %bitcast_dynamic-update-slice_fusion.24 = f32[5,1,80,4480]{3,2,1,0:T(8,128)} fusion(f32[5,1,80,4480]{3,2,1,0:T(8,128)} %get-tuple-element.619, s32[]{:T(128)} %get-tuple-element.618, f32[1,80,4480]{2,1,0:T(8,128)S(1)} %fusion.121, f32[]{:T(128)} %bitcast.266, f32[]{:T(128)} %bitcast.267, f32[]{:T(128)} %bitcast.268, f32[]{:T(128)} %bitcast.269, ...), kind=kLoop, calls=%fused_computation.22.clone.1 | loop fusion | flops 7526400 | bytes 2873344 | tf_op jit(solution)/shard_map/while/body/jit(dynamic_update_index_in_dim)/dynamic_update_slice | solution.py:61
  (195 shorter events, 276.6 us)
Async XLA Ops:
  7.2 82.1 %all-gather.3.cloned.1.call-start = ((), (), s32[]{:S(2)}) async-start(), calls=%async_computation | async-start | bytes 2433024 | tf_op jit(solution)/shard_map/all_gather | solution.py:80
  92.0 2.3 copy-start
  277.0 21.6 %collective-permute-start.8 = (f32[2,5,280]{2,1,0:T(8,128)S(1)}, f32[2,5,280]{2,1,0:T(8,128)S(1)}, u32[]{:S(2)}, u32[]{:S(2)}) collective-permute-start(f32[2,5,280]{2,1,0:T(8,128)S(1)} %add_multiply_fusion.3), channel_id=1, source_target_pairs={{0,1},{1,2},{2,3},{3,4},{4,5},{5,6},{6,7},{8,9},{9,10},{10,11},{11... | collective-permute-start | bytes 33608 | tf_op jit(solution)/shard_map/ppermute | solution.py:15
  284.2 16.3 %collective-permute-start.9 = (f32[2,5,280]{2,1,0:T(8,128)S(1)}, f32[2,5,280]{2,1,0:T(8,128)S(1)}, u32[]{:S(2)}, u32[]{:S(2)}) collective-permute-start(f32[2,5,280]{2,1,0:T(8,128)S(1)} %add_multiply_fusion.3), channel_id=1, source_target_pairs={{1,0},{2,1},{3,2},{4,3},{5,4},{6,5},{7,6},{9,8},{10,9},{11,10},{12... | collective-permute-start | bytes 33608 | tf_op jit(solution)/shard_map/ppermute | solution.py:18
  289.3 97.2 %collective-permute-start.6 = (f32[2,5,560]{2,1,0:T(8,128)S(1)}, f32[2,5,560]{2,1,0:T(8,128)S(1)}, u32[]{:S(2)}, u32[]{:S(2)}) collective-permute-start(f32[2,5,560]{2,1,0:T(8,128)S(1)} %get-tuple-element.376), channel_id=1, source_target_pairs={{0,1},{1,2},{2,3},{3,4},{4,5},{5,6},{6,7},{8,9},{9,10},{10,11},{11... | collective-permute-start | bytes 67208 | tf_op jit(solution)/shard_map/ppermute | solution.py:15
  293.0 95.5 %collective-permute-start.7 = (f32[2,5,560]{2,1,0:T(8,128)S(1)}, f32[2,5,560]{2,1,0:T(8,128)S(1)}, u32[]{:S(2)}, u32[]{:S(2)}) collective-permute-start(f32[2,5,560]{2,1,0:T(8,128)S(1)} %get-tuple-element.377), channel_id=1, source_target_pairs={{1,0},{2,1},{3,2},{4,3},{5,4},{6,5},{7,6},{9,8},{10,9},{11,10},{12... | collective-permute-start | bytes 67208 | tf_op jit(solution)/shard_map/ppermute | solution.py:18
  294.9 182.8 %collective-permute-start.4 = (f32[2,5,1120]{2,1,0:T(8,128)}, f32[2,5,1120]{2,1,0:T(8,128)}, u32[]{:S(2)}, u32[]{:S(2)}) collective-permute-start(f32[2,5,1120]{2,1,0:T(8,128)} %get-tuple-element.374), channel_id=1, source_target_pairs={{0,1},{1,2},{2,3},{3,4},{4,5},{5,6},{6,7},{8,9},{9,10},{10,11},{11... | collective-permute-start | bytes 134408 | tf_op jit(solution)/shard_map/ppermute | solution.py:15
  298.6 181.0 %collective-permute-start.5 = (f32[2,5,1120]{2,1,0:T(8,128)S(1)}, f32[2,5,1120]{2,1,0:T(8,128)}, u32[]{:S(2)}, u32[]{:S(2)}) collective-permute-start(f32[2,5,1120]{2,1,0:T(8,128)S(1)} %get-tuple-element.375), channel_id=1, source_target_pairs={{1,0},{2,1},{3,2},{4,3},{5,4},{6,5},{7,6},{9,8},{10,9},{11,10},{12... | collective-permute-start | bytes 134408 | tf_op jit(solution)/shard_map/ppermute | solution.py:18
  300.5 279.2 %collective-permute-start.2 = (f32[2,5,2240]{2,1,0:T(8,128)}, f32[2,5,2240]{2,1,0:T(8,128)}, u32[]{:S(2)}, u32[]{:S(2)}) collective-permute-start(f32[2,5,2240]{2,1,0:T(8,128)} %get-tuple-element.372), channel_id=1, source_target_pairs={{0,1},{1,2},{2,3},{3,4},{4,5},{5,6},{6,7},{8,9},{9,10},{10,11},{11... | collective-permute-start | bytes 268808 | tf_op jit(solution)/shard_map/ppermute | solution.py:15
  386.5 193.2 %collective-permute-start.3 = (f32[2,5,2240]{2,1,0:T(8,128)}, f32[2,5,2240]{2,1,0:T(8,128)}, u32[]{:S(2)}, u32[]{:S(2)}) collective-permute-start(f32[2,5,2240]{2,1,0:T(8,128)} %get-tuple-element.373), channel_id=1, source_target_pairs={{1,0},{2,1},{3,2},{4,3},{5,4},{6,5},{7,6},{9,8},{10,9},{11,10},{12... | collective-permute-start | bytes 268808 | tf_op jit(solution)/shard_map/ppermute | solution.py:18
  388.4 286.8 %collective-permute-start = (f32[2,5,4480]{2,1,0:T(8,128)}, f32[2,5,4480]{2,1,0:T(8,128)}, u32[]{:S(2)}, u32[]{:S(2)}) collective-permute-start(f32[2,5,4480]{2,1,0:T(8,128)} %get-tuple-element.370), channel_id=1, source_target_pairs={{0,1},{1,2},{2,3},{3,4},{4,5},{5,6},{6,7},{8,9},{9,10},{10,11},{11... | collective-permute-start | bytes 537608 | tf_op jit(solution)/shard_map/ppermute | solution.py:15
  477.7 197.5 %collective-permute-start.1 = (f32[2,5,4480]{2,1,0:T(8,128)}, f32[2,5,4480]{2,1,0:T(8,128)S(1)}, u32[]{:S(2)}, u32[]{:S(2)}) collective-permute-start(f32[2,5,4480]{2,1,0:T(8,128)} %get-tuple-element.371), channel_id=1, source_target_pairs={{1,0},{2,1},{3,2},{4,3},{5,4},{6,5},{7,6},{9,8},{10,9},{11,10},{12... | collective-permute-start | bytes 537608 | tf_op jit(solution)/shard_map/ppermute | solution.py:18
  480.7 0.9 copy-start.3
  581.2 1.6 copy-start.2
  677.1 3.3 copy-start.1
Sparse Core Ops, SparseCore 0:
  10.6 78.6 all-gather.2
where the time goes:
time: 818 us; the launch traced here: 805 us
  other arithmetic  421 us (51%)
  local copies, waits for them, and re-layouts  256 us (31%)
  waiting for transfers between devices  80.7 us (10%)
  starting transfers between devices  31.4 us (4%)
  between operations  15 us (2%)
    add x25, other arithmetic, smooth(): vertical + weights[tap_index] * padded[..., tap_index:tap_index + row_cou...  185 us
    broadcast_in_dim x20, other arithmetic, level_maps(): moments = lax.map(lambda field: smooth(field, weights), stacked)  107 us
    dynamic_update_slice x10, other arithmetic, level_maps(): moments = lax.map(lambda field: smooth(field, weights), stacked)  101 us
    all_gather x1, waiting for transfers between devices, local(): truth_rows = lax.all_gather(truth_field, 'samp', axis=1, tiled=True)  80 us
    slice x4, local copies, waits for them, and re-layouts, halve_grid(): lower[..., 1::2]  39.5 us
    slice x4, local copies, waits for them, and re-layouts, halve_grid(): upper[..., 1::2]  39.1 us
    slice x4, local copies, waits for them, and re-layouts, halve_grid(): lower[..., 0::2]  39.1 us
    slice x4, local copies, waits for them, and re-layouts, halve_grid(): upper[..., 0::2] + upper[..., 1::2] + lower[..., 0::2] + lower[..., 1::2]  38.2 us
  transfers between devices with their start and end apart: 11, of which 1 were waited for; matrix products, arithmetic and copies ran while one was open for 45% of the time, Pallas kernels for 0%

commit v1 on v0

--- a/solution.py
+++ b/solution.py
@@ -77,7 +77,9 @@
     weights = window()
     truth_levels = []
     sample_levels = []
-    truth_rows = lax.all_gather(truth_field, "samp", axis=1, tiled=True)
+    truth_rows = jnp.concatenate(
+        lax.all_to_all(jnp.stack([truth_field] * lax.axis_size("samp")), "samp", 0, 0), axis=1
+    )
     current = jnp.concatenate([truth_rows[None], samples], axis=0)
     for level_index in range(5):
         if level_index > 0:

time: 818 us -> 792 us (0.968)
  waiting for transfers between devices: 80.7 us -> 52.6 us
  between operations: 15 us -> 1.59 us
  starting transfers between devices: 31.4 us -> 41.9 us
    all_gather x1 -> x0, waiting for transfers between devices: 80 us -> none  [local(): truth_rows = lax.all_gather(truth_field, 'samp', axis=1, tiled=True)]
    all_to_all x0 -> x1, waiting for transfers between devices: none -> 52.6 us  [local(): lax.all_to_all(jnp.stack([truth_field] * lax.axis_size('samp')), 'samp',...]
    all_to_all x0 -> x1, starting transfers between devices: none -> 12 us  [local(): lax.all_to_all(jnp.stack([truth_field] * lax.axis_size('samp')), 'samp',...]
  transfers between devices with their start and end apart: 11 -> 11, of which waited for: 1 -> 1; matrix products, arithmetic and copies ran while one was open for 45% -> 47% of each run, Pallas kernels for 0% -> 0%
where the time goes in v1:
time: 792 us; the launch traced here: 778 us
  other arithmetic  424 us (54%)
  local copies, waits for them, and re-layouts  257 us (32%)
  waiting for transfers between devices  52.6 us (7%)
  starting transfers between devices  41.9 us (5%)
    add x25, other arithmetic, smooth(): vertical + weights[tap_index] * padded[..., tap_index:tap_index + row_cou...  187 us
    broadcast_in_dim x20, other arithmetic, level_maps(): moments = lax.map(lambda field: smooth(field, weights), stacked)  108 us
    dynamic_update_slice x10, other arithmetic, level_maps(): moments = lax.map(lambda field: smooth(field, weights), stacked)  102 us
    all_to_all x1, waiting for transfers between devices, local(): lax.all_to_all(jnp.stack([truth_field] * lax.axis_size('samp')), 'samp',...  52.6 us
    slice x4, local copies, waits for them, and re-layouts, halve_grid(): lower[..., 1::2]  39.5 us
    slice x4, local copies, waits for them, and re-layouts, halve_grid(): upper[..., 1::2]  39.1 us
    slice x4, local copies, waits for them, and re-layouts, halve_grid(): lower[..., 0::2]  39.1 us
    slice x4, local copies, waits for them, and re-layouts, halve_grid(): upper[..., 0::2] + upper[..., 1::2] + lower[..., 0::2] + lower[..., 1::2]  38.2 us
  transfers between devices with their start and end apart: 11, of which 1 were waited for; matrix products, arithmetic and copies ran while one was open for 47% of the time, Pallas kernels for 0%

profile of v1, /device:TPU:1, one launch (start us, length us, event | category | flops | bytes accessed | tf_op | source)
XLA Modules:
  0.0 777.8 jit_solution(13866688835884828556)
XLA Ops:
  3.2 12.0 %all-to-all-start = ((f32[32,80,140]{1,2,0:T(8,128)}), f32[32,80,140]{1,2,0:T(8,128)S(1)}, u32[]{:S(2)}, u32[]{:S(2)}) async-start(f32[32,80,140]{1,2,0:T(8,128)} %stack.52), calls=%async_computation | async-start | bytes 4718592 | tf_op jit(solution)/shard_map/all_to_all | solution.py:81
  16.6 52.6 %all-to-all-done = f32[32,80,140]{1,2,0:T(8,128)S(1)} async-done(((f32[32,80,140]{1,2,0:T(8,128)}), f32[32,80,140]{1,2,0:T(8,128)S(1)}, u32[]{:S(2)}, u32[]{:S(2)}) %all-to-all-start) | async-done | bytes 1433632 | tf_op jit(solution)/shard_map/all_to_all | solution.py:81
  74.7 7.6 slice.1230
  82.4 30.2 %slice.1231 = f32[2,40,2240]{2,1,0:T(8,128)} slice(f32[2,40,4480]{2,1,0:T(8,128)} %slice.1230), slice={[0:2:1], [0:40:1], [0:4480:2]} | slice | bytes 1433600 | tf_op jit(solution)/shard_map/slice | solution.py:46
  112.5 30.2 %slice.1232 = f32[2,40,2240]{2,1,0:T(8,128)} slice(f32[2,40,4480]{2,1,0:T(8,128)} %slice.1230), slice={[0:2:1], [0:40:1], [1:4480:2]} | slice | bytes 1433600 | tf_op jit(solution)/shard_map/slice | solution.py:46
  142.7 7.6 slice.1233
  150.3 30.4 %slice.1234 = f32[2,40,2240]{2,1,0:T(8,128)} slice(f32[2,40,4480]{2,1,0:T(8,128)} %slice.1233), slice={[0:2:1], [0:40:1], [0:4480:2]} | slice | bytes 1433600 | tf_op jit(solution)/shard_map/slice | solution.py:46
  180.7 30.2 %slice.1235 = f32[2,40,2240]{2,1,0:T(8,128)} slice(f32[2,40,4480]{2,1,0:T(8,128)} %slice.1233), slice={[0:2:1], [0:40:1], [1:4480:2]} | slice | bytes 1433600 | tf_op jit(solution)/shard_map/slice | solution.py:46
  281.6 81.9 %while.64 = (s32[]{:T(128)}, f32[5,1,5,280]{3,0,2,1:T(8,128)}, f32[11]{0:T(128)S(1)}, f32[5,1,15,280]{3,2,1,0:T(8,128)S(1)}, s32[]{:T(128)}, /*index=5*/s32[]{:T(128)}) while((s32[]{:T(128)}, f32[5,1,5,280]{3,0,2,1:T(8,128)}, f32[11]{0:T(128)S(1)}, f32[5,1,15,280]{3,2,1,0:T(8,128)S(1)}, s32[]{:T(128)}, /*index=5*/s32[]{:T(128)}) %tuple.190), condition=%wide.region_10.11_spmd, body=%wide.region_9.10_spmd.sunk | while | flops 58802 | bytes 134653 | solution.py:61
  289.3 7.1 add_bitcast_fusion.8
  305.7 7.1 add_bitcast_fusion.8
  322.1 7.1 add_bitcast_fusion.8
  338.5 7.1 add_bitcast_fusion.8
  354.8 7.1 add_bitcast_fusion.8
  370.8 83.1 %while.63 = (s32[]{:T(128)}, f32[5,1,10,560]{3,0,2,1:T(8,128)}, f32[11]{0:T(128)S(1)}, f32[5,1,20,560]{3,2,1,0:T(8,128)S(1)}, s32[]{:T(128)}, /*index=5*/s32[]{:T(128)}) while((s32[]{:T(128)}, f32[5,1,10,560]{3,0,2,1:T(8,128)}, f32[11]{0:T(128)S(1)}, f32[5,1,20,560]{3,2,1,0:T(8,128)S(1)}, s32[]{:T(128)}, /*index=5*/s32[]{:T(128)}) %tuple.193), condition=%wide.region_8.9_spmd, body=%wide.region_7.8_spmd.sunk | while | flops 235202 | bytes 493053 | solution.py:61
  378.6 7.1 add_bitcast_fusion.7
  395.2 7.1 add_bitcast_fusion.7
  411.8 7.1 add_bitcast_fusion.7
  428.4 7.1 add_bitcast_fusion.7
  445.0 7.1 add_bitcast_fusion.7
  460.1 95.4 %while.62 = (s32[]{:T(128)}, f32[5,1,20,1120]{3,0,2,1:T(8,128)}, f32[11]{0:T(128)S(1)}, f32[5,1,30,1120]{3,2,1,0:T(8,128)}, s32[]{:T(128)}, /*index=5*/s32[]{:T(128)}) while((s32[]{:T(128)}, f32[5,1,20,1120]{3,0,2,1:T(8,128)}, f32[11]{0:T(128)S(1)}, f32[5,1,30,1120]{3,2,1,0:T(8,128)}, s32[]{:T(128)}, /*index=5*/s32[]{:T(128)}) %tuple.199), condition=%wide.region_6.7_spmd, body=%wide.region_5.6_spmd.sunk | while | flops 940802 | bytes 1881853 | solution.py:61
  469.0 7.3 add_bitcast_fusion.6
  488.1 7.3 add_bitcast_fusion.6
  507.1 7.3 add_bitcast_fusion.6
  526.1 7.3 add_bitcast_fusion.6
  545.2 7.3 add_bitcast_fusion.6
  562.2 90.0 %while.61 = (s32[]{:T(128)}, f32[5,1,40,2240]{3,2,1,0:T(8,128)}, f32[11]{0:T(128)S(1)}, f32[5,1,50,2240]{3,2,1,0:T(8,128)}, s32[]{:T(128)}) while((s32[]{:T(128)}, f32[5,1,40,2240]{3,2,1,0:T(8,128)}, f32[11]{0:T(128)S(1)}, f32[5,1,50,2240]{3,2,1,0:T(8,128)}, s32[]{:T(128)}) %tuple.198), condition=%wide.region_4.5_spmd, body=%wide.region_3.4_spmd.sunk | while | flops 3763202 | bytes 5930181 | solution.py:61
  564.0 7.4 fusion.123
  571.4 8.8 %bitcast_dynamic-update-slice_fusion.25 = f32[5,1,40,2240]{3,2,1,0:T(8,128)} fusion(f32[5,1,40,2240]{3,2,1,0:T(8,128)} %get-tuple-element.634, s32[]{:T(128)} %get-tuple-element.633, f32[1,40,2240]{2,1,0:T(8,128)S(1)} %fusion.123, f32[]{:T(128)} %bitcast.276, f32[]{:T(128)} %bitcast.277, f32[]{:T(128)} %bitcast.278, f32[]{:T(128)} %bitcast.279, ...), kind=kLoop, calls=%fused_computation.56.clone.1 | loop fusion | flops 1881600 | bytes 733184 | tf_op jit(solution)/shard_map/while/body/jit(dynamic_update_index_in_dim)/dynamic_update_slice | solution.py:61
  581.9 7.4 fusion.123
  589.4 8.8 %bitcast_dynamic-update-slice_fusion.25 = f32[5,1,40,2240]{3,2,1,0:T(8,128)} fusion(f32[5,1,40,2240]{3,2,1,0:T(8,128)} %get-tuple-element.634, s32[]{:T(128)} %get-tuple-element.633, f32[1,40,2240]{2,1,0:T(8,128)S(1)} %fusion.123, f32[]{:T(128)} %bitcast.276, f32[]{:T(128)} %bitcast.277, f32[]{:T(128)} %bitcast.278, f32[]{:T(128)} %bitcast.279, ...), kind=kLoop, calls=%fused_computation.56.clone.1 | loop fusion | flops 1881600 | bytes 733184 | tf_op jit(solution)/shard_map/while/body/jit(dynamic_update_index_in_dim)/dynamic_update_slice | solution.py:61
  599.9 7.4 fusion.123
  607.4 8.8 %bitcast_dynamic-update-slice_fusion.25 = f32[5,1,40,2240]{3,2,1,0:T(8,128)} fusion(f32[5,1,40,2240]{3,2,1,0:T(8,128)} %get-tuple-element.634, s32[]{:T(128)} %get-tuple-element.633, f32[1,40,2240]{2,1,0:T(8,128)S(1)} %fusion.123, f32[]{:T(128)} %bitcast.276, f32[]{:T(128)} %bitcast.277, f32[]{:T(128)} %bitcast.278, f32[]{:T(128)} %bitcast.279, ...), kind=kLoop, calls=%fused_computation.56.clone.1 | loop fusion | flops 1881600 | bytes 733184 | tf_op jit(solution)/shard_map/while/body/jit(dynamic_update_index_in_dim)/dynamic_update_slice | solution.py:61
  618.0 7.4 fusion.123
  625.4 8.8 %bitcast_dynamic-update-slice_fusion.25 = f32[5,1,40,2240]{3,2,1,0:T(8,128)} fusion(f32[5,1,40,2240]{3,2,1,0:T(8,128)} %get-tuple-element.634, s32[]{:T(128)} %get-tuple-element.633, f32[1,40,2240]{2,1,0:T(8,128)S(1)} %fusion.123, f32[]{:T(128)} %bitcast.276, f32[]{:T(128)} %bitcast.277, f32[]{:T(128)} %bitcast.278, f32[]{:T(128)} %bitcast.279, ...), kind=kLoop, calls=%fused_computation.56.clone.1 | loop fusion | flops 1881600 | bytes 733184 | tf_op jit(solution)/shard_map/while/body/jit(dynamic_update_index_in_dim)/dynamic_update_slice | solution.py:61
  636.0 7.4 fusion.123
  643.4 8.8 %bitcast_dynamic-update-slice_fusion.25 = f32[5,1,40,2240]{3,2,1,0:T(8,128)} fusion(f32[5,1,40,2240]{3,2,1,0:T(8,128)} %get-tuple-element.634, s32[]{:T(128)} %get-tuple-element.633, f32[1,40,2240]{2,1,0:T(8,128)S(1)} %fusion.123, f32[]{:T(128)} %bitcast.276, f32[]{:T(128)} %bitcast.277, f32[]{:T(128)} %bitcast.278, f32[]{:T(128)} %bitcast.279, ...), kind=kLoop, calls=%fused_computation.56.clone.1 | loop fusion | flops 1881600 | bytes 733184 | tf_op jit(solution)/shard_map/while/body/jit(dynamic_update_index_in_dim)/dynamic_update_slice | solution.py:61
  659.8 112.8 %while.60 = (s32[]{:T(128)}, f32[5,1,80,4480]{3,2,1,0:T(8,128)}, f32[11]{0:T(128)S(1)}, f32[5,1,90,4480]{3,2,1,0:T(8,128)}, s32[]{:T(128)}) while((s32[]{:T(128)}, f32[5,1,80,4480]{3,2,1,0:T(8,128)}, f32[11]{0:T(128)S(1)}, f32[5,1,90,4480]{3,2,1,0:T(8,128)}, s32[]{:T(128)}) %tuple.197), condition=%wide.region_2.3_spmd, body=%wide.region_1.2_spmd.sunk | while | flops 15052802 | bytes 23302340 | solution.py:61
  662.1 8.7 %fusion.121 = f32[1,80,4480]{2,1,0:T(8,128)S(1)} fusion(f32[1,90,4480]{2,1,0:T(8,128)S(1)} %dynamic-slice_bitcast_fusion.10, f32[]{:T(128)} %bitcast.263, f32[]{:T(128)} %bitcast.264, f32[]{:T(128)} %bitcast.265, f32[]{:T(128)} %bitcast.266, f32[]{:T(128)} %bitcast.267, f32[]{:T(128)} %bitcast.268, f32[]{:T(128)} %bitcast.269, f32[]{:T(128)} %bitcast.270, ...), kind=kLoop, calls=%fused_computation.2.clone.1 | loop fusion | flops 7526400 | bytes 17203244 | tf_op jit(solution)/shard_map/while/body/eval_jaxpr/add | solution.py:34
  670.8 11.6 %bitcast_dynamic-update-slice_fusion.24 = f32[5,1,80,4480]{3,2,1,0:T(8,128)} fusion(f32[5,1,80,4480]{3,2,1,0:T(8,128)} %get-tuple-element.619, s32[]{:T(128)} %get-tuple-element.618, f32[1,80,4480]{2,1,0:T(8,128)S(1)} %fusion.121, f32[]{:T(128)} %bitcast.263, f32[]{:T(128)} %bitcast.264, f32[]{:T(128)} %bitcast.265, f32[]{:T(128)} %bitcast.266, ...), kind=kLoop, calls=%fused_computation.22.clone.1 | loop fusion | flops 7526400 | bytes 2873344 | tf_op jit(solution)/shard_map/while/body/jit(dynamic_update_index_in_dim)/dynamic_update_slice | solution.py:61
  684.7 8.7 %fusion.121 = f32[1,80,4480]{2,1,0:T(8,128)S(1)} fusion(f32[1,90,4480]{2,1,0:T(8,128)S(1)} %dynamic-slice_bitcast_fusion.10, f32[]{:T(128)} %bitcast.263, f32[]{:T(128)} %bitcast.264, f32[]{:T(128)} %bitcast.265, f32[]{:T(128)} %bitcast.266, f32[]{:T(128)} %bitcast.267, f32[]{:T(128)} %bitcast.268, f32[]{:T(128)} %bitcast.269, f32[]{:T(128)} %bitcast.270, ...), kind=kLoop, calls=%fused_computation.2.clone.1 | loop fusion | flops 7526400 | bytes 17203244 | tf_op jit(solution)/shard_map/while/body/eval_jaxpr/add | solution.py:34
  693.4 11.5 %bitcast_dynamic-update-slice_fusion.24 = f32[5,1,80,4480]{3,2,1,0:T(8,128)} fusion(f32[5,1,80,4480]{3,2,1,0:T(8,128)} %get-tuple-element.619, s32[]{:T(128)} %get-tuple-element.618, f32[1,80,4480]{2,1,0:T(8,128)S(1)} %fusion.121, f32[]{:T(128)} %bitcast.263, f32[]{:T(128)} %bitcast.264, f32[]{:T(128)} %bitcast.265, f32[]{:T(128)} %bitcast.266, ...), kind=kLoop, calls=%fused_computation.22.clone.1 | loop fusion | flops 7526400 | bytes 2873344 | tf_op jit(solution)/shard_map/while/body/jit(dynamic_update_index_in_dim)/dynamic_update_slice | solution.py:61
  707.2 8.7 %fusion.121 = f32[1,80,4480]{2,1,0:T(8,128)S(1)} fusion(f32[1,90,4480]{2,1,0:T(8,128)S(1)} %dynamic-slice_bitcast_fusion.10, f32[]{:T(128)} %bitcast.263, f32[]{:T(128)} %bitcast.264, f32[]{:T(128)} %bitcast.265, f32[]{:T(128)} %bitcast.266, f32[]{:T(128)} %bitcast.267, f32[]{:T(128)} %bitcast.268, f32[]{:T(128)} %bitcast.269, f32[]{:T(128)} %bitcast.270, ...), kind=kLoop, calls=%fused_computation.2.clone.1 | loop fusion | flops 7526400 | bytes 17203244 | tf_op jit(solution)/shard_map/while/body/eval_jaxpr/add | solution.py:34
  716.0 11.5 %bitcast_dynamic-update-slice_fusion.24 = f32[5,1,80,4480]{3,2,1,0:T(8,128)} fusion(f32[5,1,80,4480]{3,2,1,0:T(8,128)} %get-tuple-element.619, s32[]{:T(128)} %get-tuple-element.618, f32[1,80,4480]{2,1,0:T(8,128)S(1)} %fusion.121, f32[]{:T(128)} %bitcast.263, f32[]{:T(128)} %bitcast.264, f32[]{:T(128)} %bitcast.265, f32[]{:T(128)} %bitcast.266, ...), kind=kLoop, calls=%fused_computation.22.clone.1 | loop fusion | flops 7526400 | bytes 2873344 | tf_op jit(solution)/shard_map/while/body/jit(dynamic_update_index_in_dim)/dynamic_update_slice | solution.py:61
  729.8 8.7 %fusion.121 = f32[1,80,4480]{2,1,0:T(8,128)S(1)} fusion(f32[1,90,4480]{2,1,0:T(8,128)S(1)} %dynamic-slice_bitcast_fusion.10, f32[]{:T(128)} %bitcast.263, f32[]{:T(128)} %bitcast.264, f32[]{:T(128)} %bitcast.265, f32[]{:T(128)} %bitcast.266, f32[]{:T(128)} %bitcast.267, f32[]{:T(128)} %bitcast.268, f32[]{:T(128)} %bitcast.269, f32[]{:T(128)} %bitcast.270, ...), kind=kLoop, calls=%fused_computation.2.clone.1 | loop fusion | flops 7526400 | bytes 17203244 | tf_op jit(solution)/shard_map/while/body/eval_jaxpr/add | solution.py:34
  738.5 11.6 %bitcast_dynamic-update-slice_fusion.24 = f32[5,1,80,4480]{3,2,1,0:T(8,128)} fusion(f32[5,1,80,4480]{3,2,1,0:T(8,128)} %get-tuple-element.619, s32[]{:T(128)} %get-tuple-element.618, f32[1,80,4480]{2,1,0:T(8,128)S(1)} %fusion.121, f32[]{:T(128)} %bitcast.263, f32[]{:T(128)} %bitcast.264, f32[]{:T(128)} %bitcast.265, f32[]{:T(128)} %bitcast.266, ...), kind=kLoop, calls=%fused_computation.22.clone.1 | loop fusion | flops 7526400 | bytes 2873344 | tf_op jit(solution)/shard_map/while/body/jit(dynamic_update_index_in_dim)/dynamic_update_slice | solution.py:61
  752.3 8.7 %fusion.121 = f32[1,80,4480]{2,1,0:T(8,128)S(1)} fusion(f32[1,90,4480]{2,1,0:T(8,128)S(1)} %dynamic-slice_bitcast_fusion.10, f32[]{:T(128)} %bitcast.263, f32[]{:T(128)} %bitcast.264, f32[]{:T(128)} %bitcast.265, f32[]{:T(128)} %bitcast.266, f32[]{:T(128)} %bitcast.267, f32[]{:T(128)} %bitcast.268, f32[]{:T(128)} %bitcast.269, f32[]{:T(128)} %bitcast.270, ...), kind=kLoop, calls=%fused_computation.2.clone.1 | loop fusion | flops 7526400 | bytes 17203244 | tf_op jit(solution)/shard_map/while/body/eval_jaxpr/add | solution.py:34
  761.1 11.5 %bitcast_dynamic-update-slice_fusion.24 = f32[5,1,80,4480]{3,2,1,0:T(8,128)} fusion(f32[5,1,80,4480]{3,2,1,0:T(8,128)} %get-tuple-element.619, s32[]{:T(128)} %get-tuple-element.618, f32[1,80,4480]{2,1,0:T(8,128)S(1)} %fusion.121, f32[]{:T(128)} %bitcast.263, f32[]{:T(128)} %bitcast.264, f32[]{:T(128)} %bitcast.265, f32[]{:T(128)} %bitcast.266, ...), kind=kLoop, calls=%fused_computation.22.clone.1 | loop fusion | flops 7526400 | bytes 2873344 | tf_op jit(solution)/shard_map/while/body/jit(dynamic_update_index_in_dim)/dynamic_update_slice | solution.py:61
  (195 shorter events, 284.5 us)
Async XLA Ops:
  3.2 65.9 %all-to-all-start = ((f32[32,80,140]{1,2,0:T(8,128)}), f32[32,80,140]{1,2,0:T(8,128)S(1)}, u32[]{:S(2)}, u32[]{:S(2)}) async-start(f32[32,80,140]{1,2,0:T(8,128)} %stack.52), calls=%async_computation | async-start | bytes 4718592 | tf_op jit(solution)/shard_map/all_to_all | solution.py:81
  70.7 2.3 copy-start
  255.7 20.1 %collective-permute-start.8 = (f32[2,5,280]{2,1,0:T(8,128)S(1)}, f32[2,5,280]{2,1,0:T(8,128)S(1)}, u32[]{:S(2)}, u32[]{:S(2)}) collective-permute-start(f32[2,5,280]{2,1,0:T(8,128)S(1)} %add_multiply_fusion.3), channel_id=1, source_target_pairs={{0,1},{1,2},{2,3},{3,4},{4,5},{5,6},{6,7},{8,9},{9,10},{10,11},{11... | collective-permute-start | bytes 33608 | tf_op jit(solution)/shard_map/ppermute | solution.py:15
  261.5 16.3 %collective-permute-start.9 = (f32[2,5,280]{2,1,0:T(8,128)S(1)}, f32[2,5,280]{2,1,0:T(8,128)S(1)}, u32[]{:S(2)}, u32[]{:S(2)}) collective-permute-start(f32[2,5,280]{2,1,0:T(8,128)S(1)} %add_multiply_fusion.3), channel_id=1, source_target_pairs={{1,0},{2,1},{3,2},{4,3},{5,4},{6,5},{7,6},{9,8},{10,9},{11,10},{12... | collective-permute-start | bytes 33608 | tf_op jit(solution)/shard_map/ppermute | solution.py:18
  266.6 98.5 %collective-permute-start.6 = (f32[2,5,560]{2,1,0:T(8,128)S(1)}, f32[2,5,560]{2,1,0:T(8,128)S(1)}, u32[]{:S(2)}, u32[]{:S(2)}) collective-permute-start(f32[2,5,560]{2,1,0:T(8,128)S(1)} %get-tuple-element.376), channel_id=1, source_target_pairs={{0,1},{1,2},{2,3},{3,4},{4,5},{5,6},{6,7},{8,9},{9,10},{10,11},{11... | collective-permute-start | bytes 67208 | tf_op jit(solution)/shard_map/ppermute | solution.py:15
  270.3 96.8 %collective-permute-start.7 = (f32[2,5,560]{2,1,0:T(8,128)S(1)}, f32[2,5,560]{2,1,0:T(8,128)S(1)}, u32[]{:S(2)}, u32[]{:S(2)}) collective-permute-start(f32[2,5,560]{2,1,0:T(8,128)S(1)} %get-tuple-element.377), channel_id=1, source_target_pairs={{1,0},{2,1},{3,2},{4,3},{5,4},{6,5},{7,6},{9,8},{10,9},{11,10},{12... | collective-permute-start | bytes 67208 | tf_op jit(solution)/shard_map/ppermute | solution.py:18
  272.2 184.0 %collective-permute-start.4 = (f32[2,5,1120]{2,1,0:T(8,128)}, f32[2,5,1120]{2,1,0:T(8,128)}, u32[]{:S(2)}, u32[]{:S(2)}) collective-permute-start(f32[2,5,1120]{2,1,0:T(8,128)} %get-tuple-element.374), channel_id=1, source_target_pairs={{0,1},{1,2},{2,3},{3,4},{4,5},{5,6},{6,7},{8,9},{9,10},{10,11},{11... | collective-permute-start | bytes 134408 | tf_op jit(solution)/shard_map/ppermute | solution.py:15
  275.9 182.2 %collective-permute-start.5 = (f32[2,5,1120]{2,1,0:T(8,128)S(1)}, f32[2,5,1120]{2,1,0:T(8,128)}, u32[]{:S(2)}, u32[]{:S(2)}) collective-permute-start(f32[2,5,1120]{2,1,0:T(8,128)S(1)} %get-tuple-element.375), channel_id=1, source_target_pairs={{1,0},{2,1},{3,2},{4,3},{5,4},{6,5},{7,6},{9,8},{10,9},{11,10},{12... | collective-permute-start | bytes 134408 | tf_op jit(solution)/shard_map/ppermute | solution.py:18
  277.8 281.2 %collective-permute-start.2 = (f32[2,5,2240]{2,1,0:T(8,128)}, f32[2,5,2240]{2,1,0:T(8,128)}, u32[]{:S(2)}, u32[]{:S(2)}) collective-permute-start(f32[2,5,2240]{2,1,0:T(8,128)} %get-tuple-element.372), channel_id=1, source_target_pairs={{0,1},{1,2},{2,3},{3,4},{4,5},{5,6},{6,7},{8,9},{9,10},{10,11},{11... | collective-permute-start | bytes 268808 | tf_op jit(solution)/shard_map/ppermute | solution.py:15
  365.1 193.9 %collective-permute-start.3 = (f32[2,5,2240]{2,1,0:T(8,128)}, f32[2,5,2240]{2,1,0:T(8,128)}, u32[]{:S(2)}, u32[]{:S(2)}) collective-permute-start(f32[2,5,2240]{2,1,0:T(8,128)} %get-tuple-element.373), channel_id=1, source_target_pairs={{1,0},{2,1},{3,2},{4,3},{5,4},{6,5},{7,6},{9,8},{10,9},{11,10},{12... | collective-permute-start | bytes 268808 | tf_op jit(solution)/shard_map/ppermute | solution.py:18
  367.1 287.5 %collective-permute-start = (f32[2,5,4480]{2,1,0:T(8,128)}, f32[2,5,4480]{2,1,0:T(8,128)}, u32[]{:S(2)}, u32[]{:S(2)}) collective-permute-start(f32[2,5,4480]{2,1,0:T(8,128)} %get-tuple-element.370), channel_id=1, source_target_pairs={{0,1},{1,2},{2,3},{3,4},{4,5},{5,6},{6,7},{8,9},{9,10},{10,11},{11... | collective-permute-start | bytes 537608 | tf_op jit(solution)/shard_map/ppermute | solution.py:15
  456.2 198.3 %collective-permute-start.1 = (f32[2,5,4480]{2,1,0:T(8,128)}, f32[2,5,4480]{2,1,0:T(8,128)S(1)}, u32[]{:S(2)}, u32[]{:S(2)}) collective-permute-start(f32[2,5,4480]{2,1,0:T(8,128)} %get-tuple-element.371), channel_id=1, source_target_pairs={{1,0},{2,1},{3,2},{4,3},{5,4},{6,5},{7,6},{9,8},{10,9},{11,10},{12... | collective-permute-start | bytes 537608 | tf_op jit(solution)/shard_map/ppermute | solution.py:18
  459.2 0.9 copy-start.3
  560.6 1.6 copy-start.2
  656.5 3.3 copy-start.1
